TPU v7x, 32 devices: a whole 2x2x4 slice. The times are simulated.
32 devices in a mesh: rep: 2 (over y), seg: 16 (over z, x, core).
Axes of the slice: x: 2, y: 2, z: 4, core: 2. Of those that a mesh axis runs over, the one named last changes fastest.
Arguments:
- initial: bfloat16 [32, 256, 128], P('rep'), parts along dimension 0, may hold values from -6 to 6
- left_env: bfloat16 [96, 16, 256, 256], P(('rep', 'seg')), parts along dimension 0, may hold values from -0.375 to 0.375
- partner_right: bfloat16 [96, 16, 128, 128], P(('rep', 'seg')), parts along dimension 0, may hold values from -0.5 to 0.5
- term_coef: float32 [96], P(('rep', 'seg')), parts along dimension 0, may hold values from 0.02 to 0.2
- term_source: int32 [96, 16], P('rep'), parts along dimension 0, may hold values from 0 to 15
- sector_rows: int32 [32], P('rep'), parts along dimension 0, may hold values from 64 to 256, as said below
Outputs:
- last_image: bfloat16 [8192, 128], P(('rep', 'seg')), parts along dimension 0
- projected: float32 [6, 3], P('rep'), parts along dimension 0
There are 2 independent parts, one for each index of `rep`. A program takes and returns all parts, laid end to end along the dimension named above; each array names one. Nothing has to cross between parts.
Inputs may be any that keep to these rules, and one draw needn't show every extreme that they name: `sector_rows`: every value is a multiple of 64, and at least one block has exactly 256 live rows.
All inputs are finite; a program needn't handle non-finite values.
Results may differ from a plain program's by a relative error of at most 0.0095.
Values may be sent and summed in bfloat16 or wider, within the bound.
A program may use at most 64 MiB of HBM per device.

v0:
```python
import jax
import jax.numpy as jnp
from jax import lax
from jax.sharding import PartitionSpec as P

MATVECS = 3


epsilon = 1e-06


def from_partner(value, axis, apart):
    mask = 2**apart
    pairs = [(source, source ^ mask) for source in range(lax.axis_size(axis))]
    return lax.ppermute(value, axis, pairs)


def on_device(initial, left_env, partner_right, term_coef, term_source, sector_rows):
    sectors, block_rows, block_cols = initial.shape
    total_rows = sectors * block_rows
    terms_here = left_env.shape[0]
    entries = float(total_rows * block_cols)
    device = lax.axis_index("seg")
    row_share = total_rows // lax.axis_size("seg")
    live = (
        (lax.broadcasted_iota(jnp.int32, (sectors, block_rows), 1) < sector_rows[:, None])
        .astype(jnp.float32)
        .reshape(total_rows, 1)
    )
    own_sources = lax.dynamic_slice_in_dim(term_source, device * terms_here, terms_here, 0)
    right_env = from_partner(partner_right, "seg", 0)
    start = initial.reshape(total_rows, block_cols).astype(jnp.float32) * live
    (start_square,) = (jnp.sum(start * start),)
    basis = [(start * lax.rsqrt(start_square / entries + epsilon)).astype(jnp.bfloat16)]
    images = []
    for step in range(MATVECS):
        blocks = basis[step].reshape(sectors, block_rows, block_cols)
        moved = jnp.einsum(
            "tsab,tscb->tsac", blocks[own_sources], right_env, preferred_element_type=jnp.float32
        ).astype(jnp.bfloat16)
        terms = jnp.einsum("tsij,tsjc->tsic", left_env, moved, preferred_element_type=jnp.float32)
        combined = jnp.sum(terms * term_coef[:, None, None, None], axis=0)
        image = lax.psum(combined.reshape(total_rows, block_cols) * live, "seg")
        images.append(image)
        if step + 1 < MATVECS:
            correlations = tuple((jnp.sum(vector.astype(jnp.float32) * image) for vector in basis))
            residual = image
            for vector, correlation in zip(basis, correlations):
                residual = residual - correlation / entries * vector.astype(jnp.float32)
            (residual_square,) = (jnp.sum(residual * residual),)
            basis.append(
                (residual * lax.rsqrt(residual_square / entries + epsilon)).astype(jnp.bfloat16)
            )
    values = tuple(
        (jnp.sum(vector.astype(jnp.float32) * image) for vector in basis for image in images)
    )
    projected = jnp.stack(values).reshape(MATVECS, MATVECS) / entries
    return (
        lax.dynamic_slice_in_dim(images[-1], device * row_share, row_share, 0).astype(jnp.bfloat16),
        projected,
    )


def solution(mesh):
    return jax.shard_map(
        on_device,
        mesh=mesh,
        in_specs=(
            P("rep", None, None),
            P(("rep", "seg"), None, None, None),
            P(("rep", "seg"), None, None, None),
            P(("rep", "seg")),
            P("rep", None),
            P("rep"),
        ),
        out_specs=(P(("rep", "seg"), None), P("rep", None)),
        check_vma=False,
    )
```

profile of v0, /device:TPU:0, one launch (start us, length us, event | category | flops | bytes accessed | tf_op | source)
XLA Modules:
  0.0 395.1 jit_solution(2445646033721050751)
XLA Ops:
  7.2 0.5 collective-permute-start
  7.7 0.8 compare_select_fusion
  8.6 0.1 reshape.65
  8.7 0.7 fusion.33
  9.4 2.3 multiply_reduce_fusion.5
  12.5 1.8 multiply_convert_fusion.2
  14.2 2.7 gather_fusion
  17.0 8.7 %multiply_reduce_fusion.2 = f32[16,128,256]{2,1,0:T(8,128)} fusion(f32[3]{0:T(128)S(1)} %copy-done.3, bf16[3,16,256,256]{3,2,1,0:T(8,128)(2,1)} %param.7, bf16[3,16,256,128]{3,2,1,0:T(8,128)(2,1)} %bitcast.57, bf16[3,16,128,128]{3,2,1,0:T(8,128)(2,1)S(1)} %collective-permute-done), kind=kOutput, calls=%fused_computation.5 | convolution fusion | flops 1212153856 | bytes 13107212 | tf_op jit(solution)/shard_map/tsij,tsjc->tsic/dot_general | solution.py:41
  25.6 1.9 copy.12
  27.5 2.0 bitcast_multiply_fusion.3
  29.6 100.3 %all-reduce.4.cloned.1.call-done = f32[4096,128]{1,0:T(8,128)} async-done(((f32[4096,128]{1,0:T(8,128)}), f32[4096,128]{1,0:T(8,128)}) %all-reduce.4.cloned.1.call-update) | async-done | bytes 2097168 | tf_op jit(solution)/shard_map/psum | solution.py:43
  129.9 2.7 fusion.19
  133.3 1.3 multiply_reduce_fusion.4
  135.3 2.0 multiply_convert_fusion.1
  137.2 2.7 gather_fusion.1
  140.0 8.7 %multiply_reduce_fusion.1 = f32[16,128,256]{2,1,0:T(8,128)} fusion(f32[3]{0:T(128)S(1)} %copy-done.3, bf16[3,16,256,256]{3,2,1,0:T(8,128)(2,1)} %param.7, bf16[3,16,256,128]{3,2,1,0:T(8,128)(2,1)} %bitcast.59, bf16[3,16,128,128]{3,2,1,0:T(8,128)(2,1)} %copy-done.2), kind=kOutput, calls=%fused_computation.4 | convolution fusion | flops 1212153856 | bytes 13107212 | tf_op jit(solution)/shard_map/tsij,tsjc->tsic/dot_general | solution.py:41
  148.7 2.9 copy.14
  151.6 3.6 bitcast_multiply_fusion.1
  155.2 0.2 all-reduce.8.cloned.1.call-start
  155.4 96.9 %all-reduce.6.cloned.1.call-done = f32[4096,128]{1,0:T(8,128)} async-done(((f32[4096,128]{1,0:T(8,128)}), f32[4096,128]{1,0:T(8,128)}) %all-reduce.6.cloned.1.call-update) | async-done | bytes 2097168 | tf_op jit(solution)/shard_map/psum | solution.py:43
  252.3 2.5 fusion.21
  256.0 2.7 multiply_reduce_fusion.3
  259.5 2.1 multiply_convert_fusion
  261.6 2.7 gather_fusion.2
  264.3 8.7 %multiply_reduce_fusion = f32[16,128,256]{2,1,0:T(8,128)} fusion(f32[3]{0:T(128)S(1)} %copy-done.3, bf16[3,16,256,256]{3,2,1,0:T(8,128)(2,1)} %param.7, bf16[3,16,256,128]{3,2,1,0:T(8,128)(2,1)} %bitcast.58, bf16[3,16,128,128]{3,2,1,0:T(8,128)(2,1)} %copy-done.2), kind=kOutput, calls=%fused_computation.3 | convolution fusion | flops 1212153856 | bytes 13107212 | tf_op jit(solution)/shard_map/tsij,tsjc->tsic/dot_general | solution.py:41
  273.1 2.9 copy.16
  276.0 3.6 bitcast_multiply_fusion
  279.6 97.2 %all-reduce.8.cloned.1.call-done = f32[4096,128]{1,0:T(8,128)} async-done(((f32[4096,128]{1,0:T(8,128)}), f32[4096,128]{1,0:T(8,128)}) %all-reduce.8.cloned.1.call-update) | async-done | bytes 2097168 | tf_op jit(solution)/shard_map/psum | solution.py:43
  376.8 4.1 %fusion.12 = (f32[]{:T(128)}, f32[]{:T(128)}, f32[]{:T(128)}, f32[]{:T(128)}, f32[]{:T(128)}, /*index=5*/f32[]{:T(128)}) fusion(f32[4096,128]{1,0:T(8,128)} %all-reduce.4.cloned.1.call-done, bf16[4096,128]{1,0:T(8,128)(2,1)S(1)} %multiply_convert_fusion, bf16[4096,128]{1,0:T(8,128)(2,1)S(1)} %multiply_convert_fusion.1, ...), kind=kLoop, calls=%fused_computation.27 | loop fusion | flops 9961466 | bytes 9453596 | tf_op jit(solution)/shard_map/reduce_sum | solution.py:55
  380.8 5.5 %stack.39 = f32[9]{0:T(128)S(1)} concatenate(f32[1]{0:T(128)} %bitcast.12, f32[1]{0:T(128)} %bitcast.13, f32[1]{0:T(128)} %bitcast.14, f32[1]{0:T(128)} %bitcast.15, f32[1]{0:T(128)} %bitcast.16, f32[1]{0:T(128)} %bitcast.17, f32[1]{0:T(128)} %bitcast.18, f32[1]{0:T(128)} %bitcast.19, f32[1]{0:T(128)} %bitcast.20), dimensions={0} | concatenate | bytes 72 | tf_op jit(solution)/shard_map/stack | solution.py:57
  386.4 0.7 div.30
  387.0 1.5 dynamic-slice_convert_fusion
  (18 shorter events, 0.3 us)
Async XLA Ops:
  7.2 122.8 %all-reduce.4.cloned.1.call-start = ((), (), s32[]{:S(2)}) async-start(), calls=%async_computation | async-start | bytes 4194304 | tf_op jit(solution)/shard_map/psum | solution.py:43
  7.2 9.8 %collective-permute-start = (bf16[3,16,128,128]{3,2,1,0:T(8,128)(2,1)}, bf16[3,16,128,128]{3,2,1,0:T(8,128)(2,1)S(1)}, u32[]{:S(2)}, u32[]{:S(2)}) collective-permute-start(bf16[3,16,128,128]{3,2,1,0:T(8,128)(2,1)} %param.8), channel_id=1, source_target_pairs={{0,1},{1,0},{2,3},{3,2},{4,5},{5,4},{6,7},{7,6},{8,9},{9,8},{10,11... | collective-permute-start | bytes 4718600 | tf_op jit(solution)/shard_map/ppermute | solution.py:15
  14.2 2.7 copy-start.3
  17.0 8.7 %copy-start.2 = (bf16[3,16,128,128]{3,2,1,0:T(8,128)(2,1)}, bf16[3,16,128,128]{3,2,1,0:T(8,128)(2,1)S(1)}, u32[]{:S(2)}) copy-start(bf16[3,16,128,128]{3,2,1,0:T(8,128)(2,1)S(1)} %collective-permute-done) | copy-start | bytes 4718596
  29.5 100.4 %copy-start = (bf16[16,256,128]{2,1,0:T(8,128)(2,1)S(1)}, bf16[16,256,128]{2,1,0:T(8,128)(2,1)}, u32[]{:S(2)}) copy-start(bf16[16,256,128]{2,1,0:T(8,128)(2,1)} %param.6) | copy-start | bytes 3145732
  29.5 222.8 %all-reduce.6.cloned.1.call-start = ((), (), s32[]{:S(2)}) async-start(), calls=%async_computation.1 | async-start | bytes 4194304 | tf_op jit(solution)/shard_map/psum | solution.py:43
  129.9 3.3 copy-start.1
  155.2 221.5 %all-reduce.8.cloned.1.call-start = ((), (), s32[]{:S(2)}) async-start(), calls=%async_computation.2 | async-start | bytes 4194304 | tf_op jit(solution)/shard_map/psum | solution.py:43
Sparse Core Ops, SparseCore 0:
  29.7 100.2 all-reduce.3
  155.3 96.9 all-reduce.5
  279.7 96.9 all-reduce.7
where the time goes:
time: 396 us; the launch traced here: 395 us
  waiting for transfers between devices  294 us (74%)
  other arithmetic  32.1 us (8%)
  matrix products  26.1 us (7%)
  local copies, waits for them, and re-layouts  23.9 us (6%)
  between operations  17.8 us (4%)
    psum x3, waiting for transfers between devices, on_device(): image = lax.psum(combined.reshape(total_rows, block_cols) * live, 'seg')  294 us
    dot_general x3, matrix products, on_device(): jnp.einsum('tsij,tsjc->tsic', left_env, moved, preferred_element_type=jnp...  26.1 us
    reduce_sum x3, other arithmetic, on_device(): jnp.sum(vector.astype(jnp.float32) * image)  9.26 us
    mul x3, other arithmetic, on_device(): image = lax.psum(combined.reshape(total_rows, block_cols) * live, 'seg')  9.12 us
    gather x3, local copies, waits for them, and re-layouts, on_device(): blocks[own_sources]  8.16 us
  transfers between devices with their start and end apart: 4, of which 3 were waited for; matrix products, arithmetic and copies ran while one was open for 2% of the time, Pallas kernels for 0%

commit v1 on v0

v1 whole, which is shorter than its diff:
```python
import functools

import jax
import jax.numpy as jnp
from jax import lax
from jax.experimental import pallas as pl
from jax.experimental.pallas import tpu as pltpu
from jax.sharding import PartitionSpec as P

MATVECS = 3
EPS = 1e-06
F32, BF16 = jnp.float32, jnp.bfloat16
MESH = pl.DeviceIdType.MESH


def bit_of(value, b):
    return lax.rem(lax.div(value, jnp.int32(2**b)), jnp.int32(2))


def orders_of(levels):
    natural = tuple(range(levels))
    if levels < 3:
        return (natural, natural)
    return (natural, (0,) + tuple(range(2, levels)) + (1,))


def place(block, order):
    levels = len(order)
    pos = 0
    for i, b in enumerate(order):
        pos = pos + bit_of(block, b) * 2 ** (levels - 1 - i)
    return pos


def kernel(
    n, levels, sectors, rows, cols, terms,
    source_ref, coef_ref, live_ref, initial_ref, left_hbm, right_hbm,
    image_ref, projected_ref,
    left, right, basis, partial_a, partial_b, gather_a, gather_b,
    first_a, first_b, send_a, send_b, recv_a, recv_b, sum_a, sum_b,
    dots_send, dots_recv,
    left_sem, right_send, right_recv,
    rs_send, rs_recv, ag_send, ag_recv, dot_send_sem, dot_recv_sem,
):
    me = lax.axis_index("seg")
    rep = lax.axis_index("rep")
    total = sectors * rows
    half = total // (2 * n)
    entries = float(total * cols)
    per_sector = max(1, n // sectors)
    orders = orders_of(levels)
    partial = (partial_a, partial_b)
    gathered = (gather_a, gather_b)
    first = (first_a, first_b)
    sends = (send_a, send_b)
    recvs = (recv_a, recv_b)
    sums = (sum_a, sum_b)

    def peer_of(b):
        return me + (1 - 2 * bit_of(me, b)) * 2**b

    def target(b):
        return (rep, peer_of(b))

    left_copy = pltpu.make_async_copy(left_hbm, left, left_sem)
    left_copy.start()

    barrier = pltpu.get_barrier_semaphore()
    for b in range(levels):
        pl.semaphore_signal(barrier, inc=1, device_id=target(b), device_id_type=MESH)
    pl.semaphore_wait(barrier, levels)

    right_copy = pltpu.make_async_remote_copy(
        right_hbm, right, right_send, right_recv, device_id=target(0), device_id_type=MESH
    )
    right_copy.start()

    def row_mask(s):
        return lax.broadcasted_iota(jnp.int32, (rows, cols), 0) < live_ref[s]

    def fold8(x):
        return jnp.sum(x.reshape(rows // 8, 8, cols), axis=0)

    def square_body(s, acc):
        x = jnp.where(row_mask(s), initial_ref[s].astype(F32), 0.0)
        return acc + fold8(x * x)

    squares = lax.fori_loop(0, sectors, square_body, jnp.zeros((8, cols), F32))
    start_scale = lax.rsqrt(jnp.sum(squares) / entries + EPS)

    def start_body(s, carry):
        x = jnp.where(row_mask(s), initial_ref[s].astype(F32), 0.0)
        basis[0, s] = (x * start_scale).astype(BF16)
        return carry

    lax.fori_loop(0, sectors, start_body, 0)

    left_copy.wait()
    right_copy.wait()

    scales = [jnp.float32(1.0)]
    values = {}
    for k in range(MATVECS):
        last = k == MATVECS - 1
        pairs = [(j, k) for j in range(k + 1)] + [(k, i) for i in range(k)]
        scale = scales[k]

        def sector_body(s, carry, k=k, pairs=pairs, scale=scale):
            acc = jnp.zeros((rows, cols), F32)
            for t in range(terms):
                src = source_ref[me * terms + t, s]
                block = basis[k, src]
                moved = lax.dot_general(
                    block, right[t, s], (((1,), (1,)), ((), ())), preferred_element_type=F32
                ).astype(BF16)
                acc = acc + coef_ref[t] * jnp.dot(left[t, s], moved, preferred_element_type=F32)
            acc = jnp.where(row_mask(s), acc * scale, 0.0)
            if n >= sectors:
                for i in range(per_sector):
                    block_id = s * per_sector + i
                    for p in range(2):
                        piece = acc[(2 * i + p) * half:(2 * i + p + 1) * half]
                        at = pl.ds(pl.multiple_of(place(block_id, orders[p]) * half, half), half)
                        partial[p][k, at, :] = piece
                        first[p][at, :] = piece.astype(BF16)
            out = []
            for (j, i), total_here in zip(pairs, carry):
                vec = basis[j, s].astype(F32)
                if i == k:
                    out.append(total_here + fold8(vec * acc))
                else:
                    for q in range(per_sector):
                        block_id = s * per_sector + q
                        for p in range(2):
                            at = pl.ds(pl.multiple_of(place(block_id, orders[p]) * half, half), half)
                            prod = vec[(2 * q + p) * half:(2 * q + p + 1) * half] * partial[p][i, at, :]
                            total_here = total_here + jnp.sum(prod.reshape(half // 8, 8, cols), axis=0)
                    out.append(total_here)
            return tuple(out)

        dots = lax.fori_loop(
            0, sectors, sector_body, tuple(jnp.zeros((8, cols), F32) for _ in pairs)
        )
        tile = jnp.concatenate(
            [jnp.sum(d, axis=0, keepdims=True) for d in dots]
            + [jnp.zeros((8 - len(pairs), cols), F32)],
            axis=0,
        )

        def rs_copy(p, i, k=k):
            b = orders[p][i]
            size = total // 2 // 2 ** (i + 1)
            if i == 0:
                start = (1 - bit_of(me, b)) * size
                src = first[p].at[pl.ds(pl.multiple_of(start, half), size), :]
            else:
                src = sends[p].at[pl.ds(offsets[i], size), :]
            return pltpu.make_async_remote_copy(
                src, recvs[p].at[k, pl.ds(offsets[i], size), :],
                rs_send.at[k, p, i], rs_recv.at[k, p, i],
                device_id=target(b), device_id_type=MESH,
            )

        def dot_copy(i, k=k):
            return pltpu.make_async_remote_copy(
                dots_send.at[k, i], dots_recv.at[k, i],
                dot_send_sem.at[k, i], dot_recv_sem.at[k, i],
                device_id=target(i), device_id_type=MESH,
            )

        offsets = [total // 2 - total // 2 // 2**i for i in range(levels + 1)]
        pending = [rs_copy(0, 0), rs_copy(1, 0)]
        dots_send[k, 0] = tile
        dot_pending = dot_copy(0)
        pending[0].start()
        pending[1].start()
        dot_pending.start()
        final = [None, None]
        for i in range(levels):
            for p in range(2):
                size = total // 2 // 2 ** (i + 1)
                b = orders[p][i]
                my = bit_of(me, b)

                def mine(begin, count, i=i, p=p, my=my, size=size, k=k):
                    at = pl.ds(pl.multiple_of(my * size + begin, half), count)
                    own = partial[p][k, at, :] if i == 0 else sums[p][
                        pl.ds(pl.multiple_of(offsets[i - 1] + my * size + begin, half), count), :]
                    other = recvs[p][k, pl.ds(pl.multiple_of(offsets[i] + begin, half), count), :]
                    return own + other.astype(F32)

                pending[p].wait()
                if i == levels - 1:
                    final[p] = mine(0, size)
                else:
                    child = size // 2
                    next_my = bit_of(me, orders[p][i + 1])
                    sends[p][pl.ds(offsets[i + 1], child), :] = mine((1 - next_my) * child, child).astype(BF16)
                    pending[p] = rs_copy(p, i + 1)
                    pending[p].start()
                    sums[p][pl.ds(pl.multiple_of(offsets[i] + next_my * child, half), child), :] = mine(next_my * child, child)
            dot_pending.wait()
            tile = tile + dots_recv[k, i]
            if i < levels - 1:
                dots_send[k, i + 1] = tile
                dot_pending = dot_copy(i + 1)
                dot_pending.start()
        for q, (j, i) in enumerate(pairs):
            values[j, i] = jnp.sum(tile[q:q + 1]) * (scales[j] / entries)
        if last:
            for p in range(2):
                image_ref[pl.ds(p * half, half), :] = final[p].astype(BF16)
            break

        ag_pending = [None, None]

        def ag_copy(p, i, k=k):
            size = total // 2 // 2 ** (i + 1)
            start = 0
            for level in range(i + 1):
                start = start + bit_of(me, orders[p][level]) * (total // 2 // 2 ** (level + 1))
            at = pl.ds(pl.multiple_of(start, half), size)
            return pltpu.make_async_remote_copy(
                gathered[p].at[k, at, :], gathered[p].at[k, at, :],
                ag_send.at[k, p, i], ag_recv.at[k, p, i],
                device_id=target(orders[p][i]), device_id_type=MESH,
            )

        for p in range(2):
            residual = final[p]
            own_sector = lax.div(me, per_sector)
            own_start = lax.rem(me, per_sector) * (2 * half) + p * half
            own_rows = pl.ds(pl.multiple_of(own_start, half), half)
            for j in range(k + 1):
                residual = residual - values[j, k] * scales[j] * basis[j, own_sector, own_rows, :].astype(F32)
            at = pl.ds(pl.multiple_of(place(me, orders[p]) * half, half), half)
            gathered[p][k, at, :] = residual.astype(BF16)
            ag_pending[p] = ag_copy(p, levels - 1)
            ag_pending[p].start()
        for i in reversed(range(levels)):
            for p in range(2):
                ag_pending[p].wait()
                if i > 0:
                    ag_pending[p] = ag_copy(p, i - 1)
                    ag_pending[p].start()

        def unpack_body(s, acc, k=k):
            for q in range(per_sector):
                block_id = s * per_sector + q
                for p in range(2):
                    at = pl.ds(pl.multiple_of(place(block_id, orders[p]) * half, half), half)
                    piece = gathered[p][k, at, :]
                    basis[k + 1, s, pl.ds((2 * q + p) * half, half), :] = piece
                    wide = piece.astype(F32)
                    acc = acc + jnp.sum((wide * wide).reshape(half // 8, 8, cols), axis=0)
            return acc

        squares = lax.fori_loop(0, sectors, unpack_body, jnp.zeros((8, cols), F32))
        scales.append(lax.rsqrt(jnp.sum(squares) / entries + EPS))

    for j in range(MATVECS):
        for i in range(MATVECS):
            projected_ref[j, i] = values[j, i]


def on_device(n, initial, left_env, partner_right, term_coef, term_source, sector_rows):
    sectors, rows, cols = initial.shape
    terms = left_env.shape[0]
    levels = n.bit_length() - 1
    total = sectors * rows
    part = total // 2
    vmem = pl.BlockSpec(memory_space=pltpu.VMEM)
    smem = pl.BlockSpec(memory_space=pltpu.SMEM)
    anym = pl.BlockSpec(memory_space=pl.ANY)
    dma = pltpu.SemaphoreType.DMA
    return pl.pallas_call(
        functools.partial(kernel, n, levels, sectors, rows, cols, terms),
        out_shape=(
            jax.ShapeDtypeStruct((total // n, cols), BF16),
            jax.ShapeDtypeStruct((MATVECS, MATVECS), F32),
        ),
        in_specs=[smem, smem, smem, vmem, anym, anym],
        out_specs=(vmem, smem),
        scratch_shapes=[
            pltpu.VMEM(left_env.shape, BF16),
            pltpu.VMEM(partner_right.shape, BF16),
            pltpu.VMEM((MATVECS, sectors, rows, cols), BF16),
            pltpu.VMEM((MATVECS, part, cols), F32),
            pltpu.VMEM((MATVECS, part, cols), F32),
            pltpu.VMEM((MATVECS - 1, part, cols), BF16),
            pltpu.VMEM((MATVECS - 1, part, cols), BF16),
            pltpu.VMEM((part, cols), BF16),
            pltpu.VMEM((part, cols), BF16),
            pltpu.VMEM((part, cols), BF16),
            pltpu.VMEM((part, cols), BF16),
            pltpu.VMEM((MATVECS, part, cols), BF16),
            pltpu.VMEM((MATVECS, part, cols), BF16),
            pltpu.VMEM((part, cols), F32),
            pltpu.VMEM((part, cols), F32),
            pltpu.VMEM((MATVECS, levels, 8, cols), F32),
            pltpu.VMEM((MATVECS, levels, 8, cols), F32),
            dma,
            dma,
            dma,
            dma((MATVECS, 2, levels)),
            dma((MATVECS, 2, levels)),
            dma((MATVECS, 2, levels)),
            dma((MATVECS, 2, levels)),
            dma((MATVECS, levels)),
            dma((MATVECS, levels)),
        ],
        compiler_params=pltpu.CompilerParams(
            collective_id=0, has_side_effects=True, vmem_limit_bytes=48 * 1024 * 1024
        ),
    )(term_source, term_coef, sector_rows, initial, left_env, partner_right)


def solution(mesh):
    return jax.shard_map(
        functools.partial(on_device, mesh.shape["seg"]),
        mesh=mesh,
        in_specs=(
            P("rep", None, None),
            P(("rep", "seg"), None, None, None),
            P(("rep", "seg"), None, None, None),
            P(("rep", "seg")),
            P("rep", None),
            P("rep"),
        ),
        out_specs=(P(("rep", "seg"), None), P("rep", None)),
        check_vma=False,
    )
```

time: 396 us -> 114 us (0.29)
  waiting for transfers between devices: 294 us -> 0 us
  Pallas kernels: 0 us -> 107 us
  other arithmetic: 32.1 us -> 0 us
  matrix products: 26.1 us -> 0 us
  local copies, waits for them, and re-layouts: 23.9 us -> 5.93 us
  between operations: 17.8 us -> 0.64 us
    psum x3 -> x0, waiting for transfers between devices: 294 us -> none  [on_device(): image = lax.psum(combined.reshape(total_rows, block_cols) * live, 'seg')]
    pallas_call x0 -> x1, Pallas kernels: none -> 107 us  [on_device(): pl.pallas_call(functools.partial(kernel, n, levels, sectors, rows, cols,...]
    dot_general x3 -> x0, matrix products: 26.1 us -> none  [on_device(): jnp.einsum('tsij,tsjc->tsic', left_env, moved, preferred_element_type=jnp...]
    reduce_sum x6 -> x0, other arithmetic: 15.7 us -> none  [the longest x3 9.26 us: on_device(): jnp.sum(vector.astype(jnp.float32) * image)]
    mul x3 -> x0, other arithmetic: 9.12 us -> none  [on_device(): image = lax.psum(combined.reshape(total_rows, block_cols) * live, 'seg')]
    gather x3 -> x0, local copies, waits for them, and re-layouts: 8.16 us -> none  [on_device(): blocks[own_sources]]
    reduce_sum x3 -> x0, local copies, waits for them, and re-layouts: 7.78 us -> none  [on_device(): combined = jnp.sum(terms * term_coef[:, None, None, None], axis=0)]
    unnamed x9 -> x11, local copies, waits for them, and re-layouts: 0.03 us -> 5.93 us
  transfers between devices with their start and end apart: 4 -> 0, of which waited for: 3 -> 0; matrix products, arithmetic and copies ran while one was open for 2% -> 0% of each run, Pallas kernels for 0% -> 0%
where the time goes in v1:
time: 114 us
  Pallas kernels  107 us (94%)
  local copies, waits for them, and re-layouts  5.93 us (5%)
    pallas_call x1, Pallas kernels, on_device(): pl.pallas_call(functools.partial(kernel, n, levels, sectors, rows, cols,...  107 us
    unnamed x11, local copies, waits for them, and re-layouts  5.93 us

profile of v1, /device:TPU:0, one launch (start us, length us, event | category | flops | bytes accessed | tf_op | source)
XLA Modules:
  0.0 113.5 jit_solution(12229560698801264821)
XLA Ops:
  0.6 0.8 copy.8.source_ref
  1.4 0.0 copy-start
  1.4 1.4 %copy-done = bf16[3,16,128,128]{3,2,1,0:T(8,128)(2,1)S(1)} copy-done((bf16[3,16,128,128]{3,2,1,0:T(8,128)(2,1)S(1)}, bf16[3,16,128,128]{3,2,1,0:T(8,128)(2,1)}, u32[]{:S(2)}) %copy-start) | copy-done | bytes 1572888
  2.8 0.0 copy-start.1
  2.8 1.2 %copy-done.1 = bf16[16,256,128]{2,1,0:T(8,128)(2,1)S(1)} copy-done((bf16[16,256,128]{2,1,0:T(8,128)(2,1)S(1)}, bf16[16,256,128]{2,1,0:T(8,128)(2,1)}, u32[]{:S(2)}) %copy-start.1) | copy-done | bytes 1048600
  4.0 0.0 copy-start.2
  4.0 0.7 copy-done.2
  4.7 0.0 copy-start.3
  4.7 0.7 copy-done.3
  5.4 107.0 %shard_map.77 = (bf16[256,128]{1,0:T(8,128)(2,1)S(1)}, f32[3,3]{1,0:T(4,128)S(1)}) custom-call(s32[48,16]{1,0:T(8,128)S(1)} %copy.8.source_ref, f32[3]{0:T(128)S(1)} %copy-done.2, s32[16]{0:T(128)S(1)} %copy-done.3, bf16[16,256,128]{2,1,0:T(8,128)(2,1)S(1)} %copy-done.1, bf16[3,16,256,256]{3,2,1,0:T(8,128)(2,1)} %left_hbm.1, ...), custom_call_target="tpu_custom_call" | custom-call | tf_op jit(solution)/shard_map/pallas_call | solution.py:276
  112.3 0.6 copy.11
  113.0 0.6 copy.12
Async XLA Ops:
  1.4 1.4 %copy-start = (bf16[3,16,128,128]{3,2,1,0:T(8,128)(2,1)S(1)}, bf16[3,16,128,128]{3,2,1,0:T(8,128)(2,1)}, u32[]{:S(2)}) copy-start(bf16[3,16,128,128]{3,2,1,0:T(8,128)(2,1)} %right_hbm.1) | copy-start | bytes 4718596
  2.8 1.2 %copy-start.1 = (bf16[16,256,128]{2,1,0:T(8,128)(2,1)S(1)}, bf16[16,256,128]{2,1,0:T(8,128)(2,1)}, u32[]{:S(2)}) copy-start(bf16[16,256,128]{2,1,0:T(8,128)(2,1)} %initial_ref.1) | copy-start | bytes 3145732
  4.0 0.7 copy-start.2
  4.7 0.7 copy-start.3

commit v2 on v0

v2 whole, which is shorter than its diff:
```python
import functools

import jax
import jax.numpy as jnp
from jax import lax
from jax.experimental import pallas as pl
from jax.experimental.pallas import tpu as pltpu
from jax.sharding import PartitionSpec as P

MATVECS = 3
EPS = 1e-06
F32, BF16 = jnp.float32, jnp.bfloat16
MESH = pl.DeviceIdType.MESH


def bit_of(value, b):
    return lax.rem(lax.div(value, jnp.int32(2**b)), jnp.int32(2))


def stages_of(levels, parts):
    groups = [(b,) for b in range(min(2, levels))]
    groups += [tuple(range(b, min(b + 2, levels))) for b in range(2, levels, 2)]
    turned = groups[:1] + groups[2:] + groups[1:2]
    return [turned if p == parts - 2 else groups for p in range(parts)]


def dot_stages_of(levels):
    return [(0,)] + [tuple(range(b, min(b + 3, levels))) for b in range(1, levels, 3)]


def group_value(device, group):
    value = 0
    for i, b in enumerate(group):
        value = value + bit_of(device, b) * 2**i
    return value


def place(block, stages, levels):
    pos, room = 0, 2**levels
    for group in stages:
        room //= 2 ** len(group)
        pos = pos + group_value(block, group) * room
    return pos


def kernel(
    n, levels, parts, sectors, rows, cols, terms,
    source_ref, coef_ref, live_ref, initial_ref, left_hbm, right_hbm,
    image_ref, projected_ref,
    left, right, basis, partial, gathered, first, sends, recvs, sums, dots_all,
    left_sem, right_send, right_recv,
    rs_send, rs_recv, ag_send, ag_recv, dot_send_sem, dot_recv_sem,
):
    me = lax.axis_index("seg")
    rep = lax.axis_index("rep")
    total = sectors * rows
    part_rows = total // parts
    piece_rows = part_rows // n
    entries = float(total * cols)
    per_sector = max(1, n // sectors)
    stages = stages_of(levels, parts)
    dot_stages = dot_stages_of(levels)

    def peer(group, diff):
        other = me
        for i, b in enumerate(group):
            if diff >> i & 1:
                other = other + (1 - 2 * bit_of(me, b)) * 2**b
        return other

    def target(group, diff):
        return (rep, peer(group, diff))

    left_copy = pltpu.make_async_copy(left_hbm, left, left_sem)
    left_copy.start()

    partners = {}
    for group in [g for part in stages for g in part] + dot_stages:
        for diff in range(1, 2 ** len(group)):
            mask = sum(2**b for i, b in enumerate(group) if diff >> i & 1)
            partners[mask] = target(group, diff)
    barrier = pltpu.get_barrier_semaphore()
    for mask in sorted(partners):
        pl.semaphore_signal(barrier, inc=1, device_id=partners[mask], device_id_type=MESH)
    pl.semaphore_wait(barrier, len(partners))

    right_copy = pltpu.make_async_remote_copy(
        right_hbm, right, right_send, right_recv, device_id=target((0,), 1), device_id_type=MESH
    )
    right_copy.start()

    def row_mask(s):
        return lax.broadcasted_iota(jnp.int32, (rows, cols), 0) < live_ref[s]

    def fold8(x):
        return jnp.sum(x.reshape(x.shape[0] // 8, 8, cols), axis=0)

    def square_body(s, acc):
        x = jnp.where(row_mask(s), initial_ref[s].astype(F32), 0.0)
        return acc + fold8(x * x)

    squares = lax.fori_loop(0, sectors, square_body, jnp.zeros((8, cols), F32))
    start_scale = lax.rsqrt(jnp.sum(squares) / entries + EPS)

    def start_body(s, carry):
        x = jnp.where(row_mask(s), initial_ref[s].astype(F32), 0.0)
        basis[0, s] = (x * start_scale).astype(BF16)
        return carry

    lax.fori_loop(0, sectors, start_body, 0)

    left_copy.wait()
    right_copy.wait()

    plan = []
    for p in range(parts):
        size, offset, steps = part_rows, 0, []
        for group in stages[p]:
            members = 2 ** len(group)
            share = size // members
            steps.append((group, members, size, share, offset))
            offset += (members - 1) * share
            size = share
        plan.append(steps)
    count = [len(steps) for steps in plan]

    def piece_at(block_id, p):
        return pl.ds(pl.multiple_of(place(block_id, stages[p], levels) * piece_rows, piece_rows), piece_rows)

    def pieces_of(s):
        for q in range(per_sector):
            for p in range(parts):
                yield p, (q * parts + p) * piece_rows, piece_at(s * per_sector + q, p)

    scales = [jnp.float32(1.0)]
    values = {}
    for k in range(MATVECS):
        last = k == MATVECS - 1
        pairs = [(j, k) for j in range(k + 1)] + [(k, i) for i in range(k)]
        scale = scales[k]
        split = n == sectors

        def rs_copies(p, i, k=k):
            group, members, size, share, offset = plan[p][i]
            out = []
            for diff in range(1, members):
                slot = offset + (diff - 1) * share
                if i == 0:
                    start = group_value(peer(group, diff), group) * share
                    src = first.at[p, pl.ds(pl.multiple_of(start, piece_rows), share), :]
                else:
                    src = sends.at[p, pl.ds(slot, share), :]
                out.append(pltpu.make_async_remote_copy(
                    src, recvs.at[k, p, pl.ds(slot, share), :],
                    rs_send.at[k, p, i, diff - 1], rs_recv.at[k, p, i, diff - 1],
                    device_id=target(group, diff), device_id_type=MESH,
                ))
            return out

        def sector_body(i, carry, k=k, pairs=pairs, scale=scale, own=0):
            s = i * 2 + (bit_of(me, 0) if own else 1 - bit_of(me, 0)) if split else i
            acc = jnp.zeros((rows, cols), F32)
            for t in range(terms):
                src = source_ref[me * terms + t, s]
                moved = lax.dot_general(
                    basis[k, src], right[t, s], (((1,), (1,)), ((), ())), preferred_element_type=F32
                ).astype(BF16)
                acc = acc + coef_ref[t] * jnp.dot(left[t, s], moved, preferred_element_type=F32)
            acc = jnp.where(row_mask(s), acc * scale, 0.0)
            for p, begin, at in pieces_of(s):
                piece = acc[begin:begin + piece_rows]
                partial[k, p, at, :] = piece
                if not (split and own):
                    first[p, at, :] = piece.astype(BF16)
            out = []
            for (j, i2), so_far in zip(pairs, carry):
                vec = basis[j, s].astype(F32)
                if i2 == k:
                    so_far = so_far + fold8(vec * acc)
                else:
                    for p, begin, at in pieces_of(s):
                        so_far = so_far + fold8(vec[begin:begin + piece_rows] * partial[i2, p, at, :])
                out.append(so_far)
            return tuple(out)

        dots = tuple(jnp.zeros((8, cols), F32) for _ in pairs)
        started = []
        pending = [None] * parts
        if split:
            dots = lax.fori_loop(0, sectors // 2, functools.partial(sector_body, own=0), dots)
        else:
            dots = lax.fori_loop(0, sectors, sector_body, dots)
        for p in range(parts):
            pending[p] = rs_copies(p, 0)
            started += pending[p]
            for copy in pending[p]:
                copy.start()
        if split:
            dots = lax.fori_loop(0, sectors // 2, functools.partial(sector_body, own=1), dots)
        tile = jnp.concatenate(
            [jnp.sum(d, axis=0, keepdims=True) for d in dots]
            + [jnp.zeros((8 - len(pairs), cols), F32)],
            axis=0,
        )

        def dot_start(i, tile, k=k):
            group = dot_stages[i]
            dots_all[k, i, 0] = tile
            out = []
            for diff in range(1, 2 ** len(group)):
                out.append(pltpu.make_async_remote_copy(
                    dots_all.at[k, i, 0], dots_all.at[k, i, diff],
                    dot_send_sem.at[k, i, diff - 1], dot_recv_sem.at[k, i, diff - 1],
                    device_id=target(group, diff), device_id_type=MESH,
                ))
                out[-1].start()
            return out

        def dot_finish(i, copies, k=k):
            group = dot_stages[i]
            for copy in copies:
                copy.wait()
            sum_here = jnp.zeros((8, cols), F32)
            for value in range(2 ** len(group)):
                slot = 0
                for q, b in enumerate(group):
                    bit = value >> q & 1
                    slot = slot + (1 - bit_of(me, b) if bit else bit_of(me, b)) * 2**q
                sum_here = sum_here + dots_all[k, i, slot]
            return sum_here

        dot_pending = dot_start(0, tile)
        dot_next = 0
        final = [None] * parts
        for i in range(max(count)):
            for p in range(parts):
                group, members, size, share, offset = plan[p][i]
                my = group_value(me, group)

                def mine(begin, length, i=i, p=p, k=k, my=my, share=share, offset=offset, members=members):
                    at = pl.ds(pl.multiple_of(my * share + begin, piece_rows), length)
                    x = partial[k, p, at, :] if i == 0 else sums[p, i - 1, at, :]
                    for diff in range(1, members):
                        slot = pl.multiple_of(offset + (diff - 1) * share + begin, piece_rows)
                        x = x + recvs[k, p, pl.ds(slot, length), :].astype(F32)
                    return x

                for copy in pending[p]:
                    copy.wait_recv()
                if i == count[p] - 1:
                    final[p] = mine(0, share)
                    continue
                next_group, next_members, _, child, next_offset = plan[p][i + 1]
                pending[p] = rs_copies(p, i + 1)
                started += pending[p]
                for diff, copy in enumerate(pending[p], 1):
                    begin = group_value(peer(next_group, diff), next_group) * child
                    slot = next_offset + (diff - 1) * child
                    sends[p, pl.ds(slot, child), :] = mine(begin, child).astype(BF16)
                    copy.start()
                begin = group_value(me, next_group) * child
                sums[p, i, pl.ds(pl.multiple_of(begin, piece_rows), child), :] = mine(begin, child)
            if dot_next < len(dot_stages):
                tile = dot_finish(dot_next, dot_pending)
                dot_next += 1
                if dot_next < len(dot_stages):
                    dot_pending = dot_start(dot_next, tile)
        for q, (j, i) in enumerate(pairs):
            values[j, i] = jnp.sum(tile[q:q + 1]) * (scales[j] / entries)
        if last:
            for p in range(parts):
                image_ref[pl.ds(p * piece_rows, piece_rows), :] = final[p].astype(BF16)
            for copy in started:
                copy.wait_send()
            break

        def ag_copies(p, i, k=k):
            group, members, size, share, offset = plan[p][i]
            start = 0
            for level in range(i + 1):
                start = start + group_value(me, plan[p][level][0]) * plan[p][level][3]
            at = pl.ds(pl.multiple_of(start, piece_rows), share)
            out = []
            for diff in range(1, members):
                out.append(pltpu.make_async_remote_copy(
                    gathered.at[k, p, at, :], gathered.at[k, p, at, :],
                    ag_send.at[k, p, i, diff - 1], ag_recv.at[k, p, i, diff - 1],
                    device_id=target(group, diff), device_id_type=MESH,
                ))
                out[-1].start()
            return out

        own_sector = lax.div(me, per_sector)
        for p in range(parts):
            residual = final[p]
            own_start = lax.rem(me, per_sector) * (parts * piece_rows) + p * piece_rows
            own_rows = pl.ds(pl.multiple_of(own_start, piece_rows), piece_rows)
            for j in range(k + 1):
                residual = residual - values[j, k] * scales[j] * basis[j, own_sector, own_rows, :].astype(F32)
            gathered[k, p, piece_at(me, p), :] = residual.astype(BF16)
            pending[p] = ag_copies(p, count[p] - 1)
            started += pending[p]
        for i in reversed(range(max(count))):
            for p in range(parts):
                for copy in pending[p]:
                    copy.wait_recv()
                if i > 0:
                    pending[p] = ag_copies(p, i - 1)
                    started += pending[p]

        def unpack_body(s, acc, k=k):
            for p, begin, at in pieces_of(s):
                piece = gathered[k, p, at, :]
                basis[k + 1, s, pl.ds(begin, piece_rows), :] = piece
                wide = piece.astype(F32)
                acc = acc + fold8(wide * wide)
            return acc

        squares = lax.fori_loop(0, sectors, unpack_body, jnp.zeros((8, cols), F32))
        scales.append(lax.rsqrt(jnp.sum(squares) / entries + EPS))
        for copy in started:
            copy.wait_send()

    for j in range(MATVECS):
        for i in range(MATVECS):
            projected_ref[j, i] = values[j, i]


def on_device(n, initial, left_env, partner_right, term_coef, term_source, sector_rows):
    sectors, rows, cols = initial.shape
    terms = left_env.shape[0]
    levels = n.bit_length() - 1
    total = sectors * rows
    parts = max(2, min(4, total // (16 * n)))
    part = total // parts
    stage_count = len(stages_of(levels, parts)[0])
    dot_count = len(dot_stages_of(levels))
    vmem = pl.BlockSpec(memory_space=pltpu.VMEM)
    smem = pl.BlockSpec(memory_space=pltpu.SMEM)
    anym = pl.BlockSpec(memory_space=pl.ANY)
    dma = pltpu.SemaphoreType.DMA
    return pl.pallas_call(
        functools.partial(kernel, n, levels, parts, sectors, rows, cols, terms),
        out_shape=(
            jax.ShapeDtypeStruct((total // n, cols), BF16),
            jax.ShapeDtypeStruct((MATVECS, MATVECS), F32),
        ),
        in_specs=[smem, smem, smem, vmem, anym, anym],
        out_specs=(vmem, smem),
        scratch_shapes=[
            pltpu.VMEM(left_env.shape, BF16),
            pltpu.VMEM(partner_right.shape, BF16),
            pltpu.VMEM((MATVECS, sectors, rows, cols), BF16),
            pltpu.VMEM((MATVECS, parts, part, cols), F32),
            pltpu.VMEM((MATVECS - 1, parts, part, cols), BF16),
            pltpu.VMEM((parts, part, cols), BF16),
            pltpu.VMEM((parts, part, cols), BF16),
            pltpu.VMEM((MATVECS, parts, part, cols), BF16),
            pltpu.VMEM((parts, stage_count, part // 2, cols), F32),
            pltpu.VMEM((MATVECS, dot_count, 8, 8, cols), F32),
            dma,
            dma,
            dma,
            dma((MATVECS, parts, stage_count, 3)),
            dma((MATVECS, parts, stage_count, 3)),
            dma((MATVECS, parts, stage_count, 3)),
            dma((MATVECS, parts, stage_count, 3)),
            dma((MATVECS, dot_count, 7)),
            dma((MATVECS, dot_count, 7)),
        ],
        compiler_params=pltpu.CompilerParams(
            collective_id=0, has_side_effects=True, vmem_limit_bytes=48 * 1024 * 1024
        ),
    )(term_source, term_coef, sector_rows, initial, left_env, partner_right)


def solution(mesh):
    return jax.shard_map(
        functools.partial(on_device, mesh.shape["seg"]),
        mesh=mesh,
        in_specs=(
            P("rep", None, None),
            P(("rep", "seg"), None, None, None),
            P(("rep", "seg"), None, None, None),
            P(("rep", "seg")),
            P("rep", None),
            P("rep"),
        ),
        out_specs=(P(("rep", "seg"), None), P("rep", None)),
        check_vma=False,
    )
```

time: 396 us -> 100 us (0.25)
  waiting for transfers between devices: 294 us -> 0 us
  Pallas kernels: 0 us -> 93.5 us
  other arithmetic: 32.1 us -> 0 us
  matrix products: 26.1 us -> 0 us
  local copies, waits for them, and re-layouts: 23.9 us -> 5.93 us
  between operations: 17.8 us -> 0.64 us
    psum x3 -> x0, waiting for transfers between devices: 294 us -> none  [on_device(): image = lax.psum(combined.reshape(total_rows, block_cols) * live, 'seg')]
    pallas_call x0 -> x1, Pallas kernels: none -> 93.5 us  [on_device(): pl.pallas_call(functools.partial(kernel, n, levels, parts, sectors, rows,...]
    dot_general x3 -> x0, matrix products: 26.1 us -> none  [on_device(): jnp.einsum('tsij,tsjc->tsic', left_env, moved, preferred_element_type=jnp...]
    reduce_sum x6 -> x0, other arithmetic: 15.7 us -> none  [the longest x3 9.26 us: on_device(): jnp.sum(vector.astype(jnp.float32) * image)]
    mul x3 -> x0, other arithmetic: 9.12 us -> none  [on_device(): image = lax.psum(combined.reshape(total_rows, block_cols) * live, 'seg')]
    gather x3 -> x0, local copies, waits for them, and re-layouts: 8.16 us -> none  [on_device(): blocks[own_sources]]
    reduce_sum x3 -> x0, local copies, waits for them, and re-layouts: 7.78 us -> none  [on_device(): combined = jnp.sum(terms * term_coef[:, None, None, None], axis=0)]
    unnamed x9 -> x11, local copies, waits for them, and re-layouts: 0.03 us -> 5.93 us
  transfers between devices with their start and end apart: 4 -> 0, of which waited for: 3 -> 0; matrix products, arithmetic and copies ran while one was open for 2% -> 0% of each run, Pallas kernels for 0% -> 0%
where the time goes in v2:
time: 100 us
  Pallas kernels  93.5 us (94%)
  local copies, waits for them, and re-layouts  5.93 us (6%)
    pallas_call x1, Pallas kernels, on_device(): pl.pallas_call(functools.partial(kernel, n, levels, parts, sectors, rows,...  93.5 us
    unnamed x11, local copies, waits for them, and re-layouts  5.93 us

profile of v2, /device:TPU:0, one launch (start us, length us, event | category | flops | bytes accessed | tf_op | source)
XLA Modules:
  0.0 100.0 jit_solution(11912798886444638847)
XLA Ops:
  0.6 0.8 copy.8.source_ref
  1.4 0.0 copy-start
  1.4 1.4 %copy-done = bf16[3,16,128,128]{3,2,1,0:T(8,128)(2,1)S(1)} copy-done((bf16[3,16,128,128]{3,2,1,0:T(8,128)(2,1)S(1)}, bf16[3,16,128,128]{3,2,1,0:T(8,128)(2,1)}, u32[]{:S(2)}) %copy-start) | copy-done | bytes 1572888
  2.8 0.0 copy-start.1
  2.8 1.2 %copy-done.1 = bf16[16,256,128]{2,1,0:T(8,128)(2,1)S(1)} copy-done((bf16[16,256,128]{2,1,0:T(8,128)(2,1)S(1)}, bf16[16,256,128]{2,1,0:T(8,128)(2,1)}, u32[]{:S(2)}) %copy-start.1) | copy-done | bytes 1048600
  4.0 0.0 copy-start.2
  4.0 0.7 copy-done.2
  4.7 0.0 copy-start.3
  4.7 0.7 copy-done.3
  5.4 93.5 %shard_map.77 = (bf16[256,128]{1,0:T(8,128)(2,1)S(1)}, f32[3,3]{1,0:T(4,128)S(1)}) custom-call(s32[48,16]{1,0:T(8,128)S(1)} %copy.8.source_ref, f32[3]{0:T(128)S(1)} %copy-done.2, s32[16]{0:T(128)S(1)} %copy-done.3, bf16[16,256,128]{2,1,0:T(8,128)(2,1)S(1)} %copy-done.1, bf16[3,16,256,256]{3,2,1,0:T(8,128)(2,1)} %left_hbm.1, ...), custom_call_target="tpu_custom_call" | custom-call | tf_op jit(solution)/shard_map/pallas_call | solution.py:342
  98.8 0.6 copy.11
  99.5 0.6 copy.12
Async XLA Ops:
  1.4 1.4 %copy-start = (bf16[3,16,128,128]{3,2,1,0:T(8,128)(2,1)S(1)}, bf16[3,16,128,128]{3,2,1,0:T(8,128)(2,1)}, u32[]{:S(2)}) copy-start(bf16[3,16,128,128]{3,2,1,0:T(8,128)(2,1)} %right_hbm.1) | copy-start | bytes 4718596
  2.8 1.2 %copy-start.1 = (bf16[16,256,128]{2,1,0:T(8,128)(2,1)S(1)}, bf16[16,256,128]{2,1,0:T(8,128)(2,1)}, u32[]{:S(2)}) copy-start(bf16[16,256,128]{2,1,0:T(8,128)(2,1)} %initial_ref.1) | copy-start | bytes 3145732
  4.0 0.7 copy-start.2
  4.7 0.7 copy-start.3

commit v3 on v2

--- a/solution.py
+++ b/solution.py
@@ -8,6 +8,7 @@
 from jax.sharding import PartitionSpec as P
 
 MATVECS = 3
+GROUP = 8
 EPS = 1e-06
 F32, BF16 = jnp.float32, jnp.bfloat16
 MESH = pl.DeviceIdType.MESH
@@ -99,7 +100,7 @@
         x = jnp.where(row_mask(s), initial_ref[s].astype(F32), 0.0)
         return acc + fold8(x * x)
 
-    squares = lax.fori_loop(0, sectors, square_body, jnp.zeros((8, cols), F32))
+    squares = lax.fori_loop(0, sectors, square_body, jnp.zeros((8, cols), F32), unroll=2)
     start_scale = lax.rsqrt(jnp.sum(squares) / entries + EPS)
 
     def start_body(s, carry):
@@ -107,7 +108,7 @@
         basis[0, s] = (x * start_scale).astype(BF16)
         return carry
 
-    lax.fori_loop(0, sectors, start_body, 0)
+    lax.fori_loop(0, sectors, start_body, 0, unroll=2)
 
     left_copy.wait()
     right_copy.wait()
@@ -157,8 +158,7 @@
                 ))
             return out
 
-        def sector_body(i, carry, k=k, pairs=pairs, scale=scale, own=0):
-            s = i * 2 + (bit_of(me, 0) if own else 1 - bit_of(me, 0)) if split else i
+        def image_of(s, k=k, scale=scale):
             acc = jnp.zeros((rows, cols), F32)
             for t in range(terms):
                 src = source_ref[me * terms + t, s]
@@ -166,37 +166,45 @@
                     basis[k, src], right[t, s], (((1,), (1,)), ((), ())), preferred_element_type=F32
                 ).astype(BF16)
                 acc = acc + coef_ref[t] * jnp.dot(left[t, s], moved, preferred_element_type=F32)
-            acc = jnp.where(row_mask(s), acc * scale, 0.0)
-            for p, begin, at in pieces_of(s):
-                piece = acc[begin:begin + piece_rows]
-                partial[k, p, at, :] = piece
-                if not (split and own):
-                    first[p, at, :] = piece.astype(BF16)
-            out = []
-            for (j, i2), so_far in zip(pairs, carry):
-                vec = basis[j, s].astype(F32)
-                if i2 == k:
-                    so_far = so_far + fold8(vec * acc)
-                else:
-                    for p, begin, at in pieces_of(s):
-                        so_far = so_far + fold8(vec[begin:begin + piece_rows] * partial[i2, p, at, :])
-                out.append(so_far)
-            return tuple(out)
+            return jnp.where(row_mask(s), acc * scale, 0.0)
+
+        def sector_body(i, carry, k=k, pairs=pairs, own=0):
+            at_once = [i * GROUP + u for u in range(GROUP)]
+            if split:
+                at_once = [x * 2 + (bit_of(me, 0) if own else 1 - bit_of(me, 0)) for x in at_once]
+            accs = [image_of(s) for s in at_once]
+            for s, acc in zip(at_once, accs):
+                for p, begin, at in pieces_of(s):
+                    piece = acc[begin:begin + piece_rows]
+                    partial[k, p, at, :] = piece
+                    if not (split and own):
+                        first[p, at, :] = piece.astype(BF16)
+                out = []
+                for (j, i2), so_far in zip(pairs, carry):
+                    vec = basis[j, s].astype(F32)
+                    if i2 == k:
+                        so_far = so_far + fold8(vec * acc)
+                    else:
+                        for p, begin, at in pieces_of(s):
+                            so_far = so_far + fold8(vec[begin:begin + piece_rows] * partial[i2, p, at, :])
+                    out.append(so_far)
+                carry = tuple(out)
+            return carry
 
         dots = tuple(jnp.zeros((8, cols), F32) for _ in pairs)
         started = []
         pending = [None] * parts
         if split:
-            dots = lax.fori_loop(0, sectors // 2, functools.partial(sector_body, own=0), dots)
+            dots = lax.fori_loop(0, sectors // 2 // GROUP, functools.partial(sector_body, own=0), dots)
         else:
-            dots = lax.fori_loop(0, sectors, sector_body, dots)
+            dots = lax.fori_loop(0, sectors // GROUP, sector_body, dots)
         for p in range(parts):
             pending[p] = rs_copies(p, 0)
             started += pending[p]
             for copy in pending[p]:
                 copy.start()
         if split:
-            dots = lax.fori_loop(0, sectors // 2, functools.partial(sector_body, own=1), dots)
+            dots = lax.fori_loop(0, sectors // 2 // GROUP, functools.partial(sector_body, own=1), dots)
         tile = jnp.concatenate(
             [jnp.sum(d, axis=0, keepdims=True) for d in dots]
             + [jnp.zeros((8 - len(pairs), cols), F32)],
@@ -316,7 +324,7 @@
                 acc = acc + fold8(wide * wide)
             return acc
 
-        squares = lax.fori_loop(0, sectors, unpack_body, jnp.zeros((8, cols), F32))
+        squares = lax.fori_loop(0, sectors, unpack_body, jnp.zeros((8, cols), F32), unroll=2)
         scales.append(lax.rsqrt(jnp.sum(squares) / entries + EPS))
         for copy in started:
             copy.wait_send()

time: 100 us -> 95 us (0.950)
  Pallas kernels: 93.5 us -> 88.2 us
    pallas_call x1, Pallas kernels: 93.5 us -> 88.2 us  [on_device(): pl.pallas_call(functools.partial(kernel, n, levels, parts, sectors, rows,...]
where the time goes in v3:
time: 95 us; the launch traced here: 94.8 us
  Pallas kernels  88.2 us (93%)
  local copies, waits for them, and re-layouts  5.93 us (6%)
    pallas_call x1, Pallas kernels, on_device(): pl.pallas_call(functools.partial(kernel, n, levels, parts, sectors, rows,...  88.2 us
    unnamed x11, local copies, waits for them, and re-layouts  5.93 us

profile of v3, /device:TPU:0, one launch (start us, length us, event | category | flops | bytes accessed | tf_op | source)
XLA Modules:
  0.0 94.8 jit_solution(13794941576905405624)
XLA Ops:
  0.6 0.8 copy.8.source_ref
  1.4 0.0 copy-start
  1.4 1.4 %copy-done = bf16[3,16,128,128]{3,2,1,0:T(8,128)(2,1)S(1)} copy-done((bf16[3,16,128,128]{3,2,1,0:T(8,128)(2,1)S(1)}, bf16[3,16,128,128]{3,2,1,0:T(8,128)(2,1)}, u32[]{:S(2)}) %copy-start) | copy-done | bytes 1572888
  2.8 0.0 copy-start.1
  2.8 1.2 %copy-done.1 = bf16[16,256,128]{2,1,0:T(8,128)(2,1)S(1)} copy-done((bf16[16,256,128]{2,1,0:T(8,128)(2,1)S(1)}, bf16[16,256,128]{2,1,0:T(8,128)(2,1)}, u32[]{:S(2)}) %copy-start.1) | copy-done | bytes 1048600
  4.0 0.0 copy-start.2
  4.0 0.7 copy-done.2
  4.7 0.0 copy-start.3
  4.7 0.7 copy-done.3
  5.4 88.2 %shard_map.77 = (bf16[256,128]{1,0:T(8,128)(2,1)S(1)}, f32[3,3]{1,0:T(4,128)S(1)}) custom-call(s32[48,16]{1,0:T(8,128)S(1)} %copy.8.source_ref, f32[3]{0:T(128)S(1)} %copy-done.2, s32[16]{0:T(128)S(1)} %copy-done.3, bf16[16,256,128]{2,1,0:T(8,128)(2,1)S(1)} %copy-done.1, bf16[3,16,256,256]{3,2,1,0:T(8,128)(2,1)} %left_hbm.1, ...), custom_call_target="tpu_custom_call" | custom-call | tf_op jit(solution)/shard_map/pallas_call | solution.py:350
  93.6 0.6 copy.11
  94.2 0.6 copy.12
Async XLA Ops:
  1.4 1.4 %copy-start = (bf16[3,16,128,128]{3,2,1,0:T(8,128)(2,1)S(1)}, bf16[3,16,128,128]{3,2,1,0:T(8,128)(2,1)}, u32[]{:S(2)}) copy-start(bf16[3,16,128,128]{3,2,1,0:T(8,128)(2,1)} %right_hbm.1) | copy-start | bytes 4718596
  2.8 1.2 %copy-start.1 = (bf16[16,256,128]{2,1,0:T(8,128)(2,1)S(1)}, bf16[16,256,128]{2,1,0:T(8,128)(2,1)}, u32[]{:S(2)}) copy-start(bf16[16,256,128]{2,1,0:T(8,128)(2,1)} %initial_ref.1) | copy-start | bytes 3145732
  4.0 0.7 copy-start.2
  4.7 0.7 copy-start.3
